TPU v7x, 512 devices: a whole 4x8x8 slice. The times are simulated.
512 devices in a mesh: rep: 16 (over z_hi, x, core), fsdp: 32 (over y, z_lo).
Axes of the slice: x: 4, y: 8, z: 8 (z_hi: 2, z_lo: 4; z = z_hi * 4 + z_lo), core: 2. Of those that a mesh axis runs over, the one named last changes fastest.
Arguments:
- activations: bfloat16 [65536, 8192], P(('rep', 'fsdp')), may hold values from -24 to 24
- queries: bfloat16 [65536, 4096], P(('rep', 'fsdp')), may hold values from -5 to 5
- keys: bfloat16 [65536, 512], P(('rep', 'fsdp')), may hold values from -5 to 5
- values: bfloat16 [65536, 512], P(('rep', 'fsdp')), may hold values from -6 to 6
- out_grad: bfloat16 [65536, 4096], P(('rep', 'fsdp')), may hold values from -3 to 3
- positions: int32 [65536], P(('rep', 'fsdp')), may hold values from 0 to 127, as said below
- shard_table: int32 [16, 32, 2], P('rep', 'fsdp'), may hold values from 0 to 8192, as said below
Outputs:
- key_grad: bfloat16 [65536, 512], P(('rep', 'fsdp'))
- weight_grad: bfloat16 [16, 32, 320, 512], P('rep', 'fsdp')
Inputs may be any that keep to these rules, and one draw needn't show every extreme that they name: shard_table[r, f] = (offset, length): device f of group r holds rows offset to offset + length - 1; in every group these runs follow f in order and cover all 8192 rows once. In all groups but one, offset = f * 256 and length = 256; in the remaining group every run lies within 128 rows of rows f * 256 to (f + 1) * 256 - 1, and some length is 320. Within each device's 128 tokens, positions count up by one from 0 at each document's first token; a device's first token has position 0.
All inputs are finite; a program needn't handle non-finite values.
Results may differ from a plain program's by a relative error of at most 0.0064.
Values may be sent and summed in bfloat16 or wider, within the bound.
A program may use at most 64 MiB of HBM per device.

v0:
```python
import math

import jax
import jax.numpy as jnp
from jax import lax
from jax.sharding import PartitionSpec as P

HEAD = 128
GROUP = 8
KV_HEADS = 4


def block_backward(queries, keys, values, out_grad, positions):
    rows_here = queries.shape[0]
    factor = 1.0 / math.sqrt(HEAD)
    query_heads = queries.reshape(rows_here, KV_HEADS, GROUP, HEAD)
    key_heads = keys.reshape(rows_here, KV_HEADS, HEAD)
    value_heads = values.reshape(rows_here, KV_HEADS, HEAD)
    grad_heads = out_grad.reshape(rows_here, KV_HEADS, GROUP, HEAD)
    scores = (
        jnp.einsum("tkgd,ukd->kgtu", query_heads, key_heads, preferred_element_type=jnp.float32)
        * factor
    )
    query_index = jnp.arange(rows_here, dtype=jnp.int32)[:, None]
    key_index = jnp.arange(rows_here, dtype=jnp.int32)[None, :]
    allowed = (key_index <= query_index) & (key_index >= query_index - positions[:, None])
    scores = jnp.where(allowed, scores, -1e30)
    largest = jnp.max(scores, axis=-1, keepdims=True)
    raised = jnp.exp(scores - largest)
    attention = raised / jnp.sum(raised, axis=-1, keepdims=True)
    attention_low = attention.astype(jnp.bfloat16)
    attended = jnp.einsum(
        "kgtu,ukd->tkgd", attention_low, value_heads, preferred_element_type=jnp.float32
    )
    row_dots = jnp.sum(grad_heads.astype(jnp.float32) * attended, axis=-1)
    prob_grads = jnp.einsum(
        "tkgd,ukd->kgtu", grad_heads, value_heads, preferred_element_type=jnp.float32
    )
    score_grads = (attention * (prob_grads - jnp.transpose(row_dots, (1, 2, 0))[..., None])).astype(
        jnp.bfloat16
    )
    value_grad = jnp.einsum(
        "kgtu,tkgd->ukd", attention_low, grad_heads, preferred_element_type=jnp.float32
    ).astype(jnp.bfloat16)
    key_grad = (
        jnp.einsum("kgtu,tkgd->ukd", score_grads, query_heads, preferred_element_type=jnp.float32)
        * factor
    ).astype(jnp.bfloat16)
    return (
        value_grad.reshape(rows_here, KV_HEADS * HEAD),
        key_grad.reshape(rows_here, KV_HEADS * HEAD),
    )


def accumulate_with(columns, incoming):
    return lax.dot_general(
        columns, incoming, (((0,), (0,)), ((), ())), preferred_element_type=jnp.float32
    )


def shards(activations, queries, keys, values, out_grad, positions, shard_table):
    value_grad, key_grad = block_backward(queries, keys, values, out_grad, positions)
    groups = lax.axis_size("fsdp")
    rows_here = activations.shape[0]
    stride = activations.shape[1] // groups
    margin = stride // 2
    width = value_grad.shape[1]
    factor = 1.0 / math.sqrt(rows_here * groups * lax.axis_size("rep"))
    device = lax.axis_index("fsdp")
    padded = jnp.pad(activations, ((0, 0), (margin, margin)))
    blocks = padded.reshape(rows_here, groups + 1, stride)
    spans = jnp.concatenate((blocks[:, :groups], blocks[:, 1:]), axis=2).reshape(
        rows_here, groups * 2 * stride
    )
    columns = lax.all_to_all(spans, "fsdp", split_axis=1, concat_axis=0, tiled=True)
    partial_value = accumulate_with(columns, lax.all_gather(value_grad, "fsdp", axis=0, tiled=True))
    window = lax.psum(partial_value, "rep")
    window = jnp.pad(window, ((0, margin), (0, 0)))
    slot_rows = stride + stride // 4
    offset = shard_table[0, 0, 0]
    length = shard_table[0, 0, 1]
    first_row = offset - (device * stride - margin)
    picked = lax.dynamic_slice_in_dim(window, first_row, slot_rows, 0)
    inside = jnp.arange(slot_rows, dtype=jnp.int32) < length
    slot_grad = jnp.where(inside[:, None], picked * factor, 0.0).astype(jnp.bfloat16)
    return (key_grad, slot_grad.reshape(1, 1, slot_rows, width))


def solution(mesh):
    return jax.shard_map(
        shards,
        mesh=mesh,
        in_specs=(
            P(("rep", "fsdp"), None),
            P(("rep", "fsdp"), None),
            P(("rep", "fsdp"), None),
            P(("rep", "fsdp"), None),
            P(("rep", "fsdp"), None),
            P(("rep", "fsdp")),
            P("rep", "fsdp", None),
        ),
        out_specs=(P(("rep", "fsdp"), None), P("rep", "fsdp", None, None)),
        check_vma=False,
    )
```

profile of v0, /device:TPU:1, one launch (start us, length us, event | category | flops | bytes accessed | tf_op | source)
XLA Modules:
  0.0 477.2 jit_solution(16399366532434216097)
XLA Ops:
  7.2 3.2 copy.34
  10.4 0.3 pad.8
  10.7 1.0 fusion.33
  11.7 2.4 pad_maximum_fusion
  14.2 0.0 copy-start
  14.2 13.7 %all-to-all-start = ((bf16[128,32,512]{0,2,1:T(8,128)(2,1)}), bf16[128,32,512]{0,2,1:T(8,128)(2,1)}, u32[]{:S(2)}, u32[]{:S(2)}) async-start(bf16[128,32,512]{0,2,1:T(8,128)(2,1)} %pad_maximum_fusion), calls=%async_computation | async-start | bytes 8388608 | tf_op jit(solution)/shard_map/all_to_all | solution.py:75
  27.9 0.0 copy-start.1
  27.9 0.0 all-gather.2.cloned.1.call-start
  28.0 0.0 copy-done
  28.0 1.3 copy.49
  29.3 0.0 copy-done.1
  29.3 0.0 copy-start.7
  29.3 0.0 copy-start.5
  29.3 0.2 copy.51
  29.6 0.0 copy-start.2
  29.6 1.0 copy.37
  30.6 0.0 copy-done.7
  30.6 0.0 copy-done.5
  30.7 0.1 copy-done.2
  30.8 2.1 fusion.35
  32.9 1.8 fusion.14
  34.8 1.1 fusion.9
  35.9 0.0 all-gather.2.cloned.1.call-update
  35.9 0.0 all-reduce.4.cloned.1.call-start
  35.9 97.1 %all-to-all-done = bf16[128,32,512]{0,2,1:T(8,128)(2,1)} async-done(((bf16[128,32,512]{0,2,1:T(8,128)(2,1)}), bf16[128,32,512]{0,2,1:T(8,128)(2,1)}, u32[]{:S(2)}, u32[]{:S(2)}) %all-to-all-start) | async-done | bytes 4194336 | tf_op jit(solution)/shard_map/all_to_all | solution.py:75
  133.0 6.5 %copy.35 = bf16[32,128,512]{2,1,0:T(8,128)(2,1)} copy(bf16[32,128,512]{1,2,0:T(8,128)(2,1)} %bitcast.13) | data formatting | bytes 8388608 | tf_op jit(solution)/shard_map/all_to_all | solution.py:75
  139.5 111.0 %all-gather.2.cloned.1.call-done = bf16[4096,512]{0,1:T(8,128)(2,1)} async-done(((bf16[128,512]{0,1:T(8,128)(2,1)}), bf16[4096,512]{0,1:T(8,128)(2,1)}) %all-gather.2.cloned.1.call-update) | async-done | bytes 4194320 | tf_op jit(solution)/shard_map/all_gather | solution.py:76
  250.4 6.8 %fusion.38 = f32[512,512]{1,0:T(8,128)} fusion(bf16[4096,512]{1,0:T(8,128)(2,1)} %bitcast.78, bf16[4096,512]{0,1:T(8,128)(2,1)} %all-gather.2.cloned.1.call-done), kind=kOutput, calls=%fused_computation.42 | convolution fusion | flops 2147483648 | bytes 9437184 | tf_op jit(solution)/shard_map/dot_general | solution.py:56
  257.3 0.0 copy-start.4
  257.3 0.0 all-reduce.4.cloned.1.call-update
  257.3 1.7 copy.29
  259.0 0.0 copy-start.3
  259.0 0.0 copy-done.4
  259.0 0.7 reshape.45
  259.7 2.1 fusion.1
  261.8 0.1 copy.31
  261.9 0.0 copy-done.3
  261.9 0.0 copy-start.6
  261.9 2.5 fusion.8
  264.3 0.8 copy.38
  265.1 0.0 copy-done.6
  265.1 0.6 fusion.34
  266.4 0.7 iota_compare_fusion.2
  267.0 201.4 %all-reduce.4.cloned.1.call-done = f32[512,512]{1,0:T(8,128)} async-done(((f32[512,512]{1,0:T(8,128)}), f32[512,512]{1,0:T(8,128)}) %all-reduce.4.cloned.1.call-update) | async-done | bytes 1048592 | tf_op jit(solution)/shard_map/psum | solution.py:77
  468.4 2.0 fusion.18
  (3 shorter events, 0.1 us)
Async XLA Ops:
  14.2 13.8 %copy-start = (bf16[128,4096]{1,0:T(8,128)(2,1)S(1)}, bf16[128,4096]{1,0:T(8,128)(2,1)}, u32[]{:S(2)}) copy-start(bf16[128,4096]{1,0:T(8,128)(2,1)} %param.8) | copy-start | bytes 3145732
  14.2 118.8 %all-to-all-start = ((bf16[128,32,512]{0,2,1:T(8,128)(2,1)}), bf16[128,32,512]{0,2,1:T(8,128)(2,1)}, u32[]{:S(2)}, u32[]{:S(2)}) async-start(bf16[128,32,512]{0,2,1:T(8,128)(2,1)} %pad_maximum_fusion), calls=%async_computation | async-start | bytes 8388608 | tf_op jit(solution)/shard_map/all_to_all | solution.py:75
  27.9 1.4 copy-start.1
  27.9 222.5 %all-gather.2.cloned.1.call-start = ((), (), s32[]{:S(2)}) async-start(), calls=%async_computation.1 | async-start | bytes 4325376 | tf_op jit(solution)/shard_map/all_gather | solution.py:76
  29.3 1.3 copy-start.7
  29.3 1.3 copy-start.5
  29.6 1.2 copy-start.2
  35.9 432.5 %all-reduce.4.cloned.1.call-start = ((), (), s32[]{:S(2)}) async-start(), calls=%async_computation.2 | async-start | bytes 2097152 | tf_op jit(solution)/shard_map/psum | solution.py:77
  257.3 1.8 copy-start.4
  259.0 2.8 copy-start.3
  261.9 3.2 copy-start.6
Sparse Core Ops, SparseCore 0:
  36.0 214.3 all-gather.1
  257.4 210.9 all-reduce.3
where the time goes:
time: 478 us; the launch traced here: 477 us
  waiting for transfers between devices  409 us (86%)
  local copies, waits for them, and re-layouts  17.7 us (4%)
  between operations  14.9 us (3%)
  matrix products  14.6 us (3%)
  starting transfers between devices  13.8 us (3%)
  other arithmetic  6.92 us (1%)
    psum x1, waiting for transfers between devices, shards(): window = lax.psum(partial_value, 'rep')  201 us
    all_gather x1, waiting for transfers between devices, shards(): lax.all_gather(value_grad, 'fsdp', axis=0, tiled=True)  111 us
    all_to_all x1, waiting for transfers between devices, shards(): lax.all_to_all(spans, 'fsdp', split_axis=1, concat_axis=0, tiled=True)  97.1 us
    all_to_all x1, starting transfers between devices, shards(): lax.all_to_all(spans, 'fsdp', split_axis=1, concat_axis=0, tiled=True)  13.7 us
  transfers between devices with their start and end apart: 3, of which 3 were waited for; matrix products, arithmetic and copies ran while one was open for 5% of the time, Pallas kernels for 0%

commit v1 on v0

v1 whole, which is shorter than its diff:
```python
import math

import jax
import jax.numpy as jnp
from jax import lax
from jax.experimental import pallas as pl
from jax.experimental.pallas import tpu as pltpu
from jax.sharding import PartitionSpec as P

HEAD = 128
GROUP = 8
KV_HEADS = 4
NX, NY, NZ, NZL, CORES = 4, 8, 8, 4, 2
RING = 8
BLOCK = 128
HALF = 64
BF16, F32 = jnp.bfloat16, jnp.float32
MESH = pl.DeviceIdType.MESH
FLOWS = (("y", 1, 0), ("y", -1, 1), ("z", 1, 2), ("z", -1, 3))


def device(x, y, z, c):
    zh, zl = z // NZL, lax.rem(z, NZL)
    return ((zh * NX + x) * CORES + c, y * NZL + zl)


def wrap(value, size):
    return lax.rem(value + 2 * size, size)


def nt_dot(a, b):
    return lax.dot_general(a, b, (((1,), (1,)), ((), ())), preferred_element_type=F32)


def kernel(
    q_ref, k_ref, v_ref, g_ref, pos_ref, acts_ref,
    key_ref, win_ref,
    acts_buf, vgt_buf, probs_buf, ring_send, ring_recv,
    zx_send, zx_recv, yx_send, yx_recv, x_send, x_recv, window,
    local_sem, acts_sems, vg_sems, ring_ssem, ring_rsem,
    zx_ssem, zx_rsem, yx_ssem, yx_rsem, x_ssem, x_rsem,
    gather_ssem, gather_rsem, spread_ssem, spread_rsem,
):
    rep, fsdp = lax.axis_index("rep"), lax.axis_index("fsdp")
    c = lax.rem(rep, CORES)
    x = lax.rem(rep // CORES, NX)
    zh = rep // (CORES * NX)
    y, zl = fsdp // NZL, lax.rem(fsdp, NZL)
    z = zh * NZL + zl
    sibling = device(x, y, z, 1 - c)
    f_count = NY * NZL
    far = lax.rem(fsdp + f_count - 1 + 2 * c, f_count)
    far_other = lax.rem(fsdp + f_count + 1 - 2 * c, f_count)

    partners = [sibling]
    partners += [device(x, wrap(y + i, NY), z, c) for i in range(1, NY)]
    partners += [device(x, y, wrap(z + i, NZ), c) for i in range(1, NZ)]
    partners += [device(wrap(x + i, NX), y, z, c) for i in range(1, NX)]
    partners += [device(wrap(x + i, NX), y, wrap(z + NZL, NZ), c) for i in range(1, NX)]
    for other in (far, far_other):
        partners += [(rep, other), (rep + 1 - 2 * c, other)]
    barrier = pltpu.get_barrier_semaphore()
    for partner in partners:
        pl.semaphore_signal(barrier, inc=1, device_id=partner, device_id_type=MESH)

    def local_acts(f):
        return pltpu.make_async_copy(
            acts_ref.at[:, pl.ds(pl.multiple_of(2 * BLOCK * f + BLOCK * c, BLOCK), BLOCK)],
            acts_buf.at[f, pl.ds(0, BLOCK)],
            local_sem.at[0],
        )

    def send_acts(f):
        return pltpu.make_async_remote_copy(
            src_ref=acts_ref.at[
                :, pl.ds(pl.multiple_of(2 * BLOCK * f + BLOCK * (1 - c), BLOCK), BLOCK)
            ],
            dst_ref=acts_buf.at[f, pl.ds(BLOCK, BLOCK)],
            send_sem=acts_sems.at[0],
            recv_sem=acts_sems.at[1],
            device_id=sibling,
            device_id_type=MESH,
        )

    @pl.loop(0, f_count)
    def _(f):
        local_acts(f).start()

    factor = 1.0 / math.sqrt(HEAD)
    key_index = lax.broadcasted_iota(jnp.int32, (BLOCK, BLOCK), 0)
    query_index = lax.broadcasted_iota(jnp.int32, (BLOCK, BLOCK), 1)
    allowed = (key_index <= query_index) & (key_index >= query_index - pos_ref[...])
    allowed = jnp.concatenate((allowed, allowed), axis=1)

    def stacked(ref, first):
        return jnp.concatenate(
            [ref[:, pl.ds(pl.multiple_of(first + i * HEAD, HEAD), HEAD)] for i in range(2)], axis=0
        )

    def values_of(g):
        keys = k_ref[:, pl.ds(pl.multiple_of(g * HEAD, HEAD), HEAD)]
        total = jnp.zeros((BLOCK, HEAD), F32)
        for pair in range(GROUP // 2):
            first = g * GROUP * HEAD + pair * 2 * HEAD
            scores = nt_dot(keys, stacked(q_ref, first)) * factor
            scores = jnp.where(allowed, scores, -1e30)
            raised = jnp.exp(scores - jnp.max(scores, axis=0, keepdims=True))
            probs = raised / jnp.sum(raised, axis=0, keepdims=True)
            probs_buf[g * (GROUP // 2) + pair] = probs
            total += jnp.dot(
                probs.astype(BF16), stacked(g_ref, first), preferred_element_type=F32
            )
        vgt_buf[pl.ds(pl.multiple_of(g * HEAD, HEAD), HEAD), pl.ds(0, BLOCK)] = total.T.astype(BF16)

    @pl.loop(0, 2)
    def _(g):
        values_of(g)

    pl.semaphore_wait(barrier, len(partners))

    @pl.loop(0, f_count)
    def _(f):
        send_acts(f).start()

    @pl.loop(2, KV_HEADS)
    def _(g):
        values_of(g)

    vg_copy = pltpu.make_async_remote_copy(
        src_ref=vgt_buf.at[:, pl.ds(0, BLOCK)],
        dst_ref=vgt_buf.at[:, pl.ds(BLOCK, BLOCK)],
        send_sem=vg_sems.at[0],
        recv_sem=vg_sems.at[1],
        device_id=sibling,
        device_id_type=MESH,
    )
    vg_copy.start()
    own_half = acts_buf.at[:, pl.ds(0, BLOCK)]
    far_half = acts_buf.at[:, pl.ds(BLOCK, BLOCK)]
    pltpu.make_async_copy(own_half, own_half, local_sem.at[0]).wait()
    pltpu.make_async_copy(far_half, far_half, acts_sems.at[1]).wait()
    vg_copy.wait_recv()

    def place(axis):
        return y if axis == "y" else z

    def ring_copy(flow, step, sub):
        axis, way, _ = FLOWS[flow]
        if axis == "y":
            target = device(x, wrap(y + way, NY), z, c)
        else:
            target = device(x, y, wrap(z + way, NZ), c)
        return pltpu.make_async_remote_copy(
            src_ref=ring_send.at[flow, step, sub],
            dst_ref=ring_recv.at[flow, step, sub],
            send_sem=ring_ssem.at[flow, step, sub],
            recv_sem=ring_rsem.at[flow, step, sub],
            device_id=target,
            device_id_type=MESH,
        )

    def partial(flow, step, sub):
        axis, way, g = FLOWS[flow]
        chunk = wrap(place(axis) - way * (1 + step), RING)
        if axis == "y":
            columns = g * HEAD + sub * HALF
            blocks = [acts_buf[chunk * NZL + i] for i in range(4)]
        else:
            columns = pl.multiple_of(g * HEAD + (chunk // NZL) * HALF, HALF)
            blocks = [acts_buf[(4 * sub + i) * NZL + lax.rem(chunk, NZL)] for i in range(4)]
        return jnp.dot(
            vgt_buf[pl.ds(columns, HALF), :],
            jnp.concatenate(blocks, axis=1),
            preferred_element_type=F32,
        )

    def ring_step(step, first):
        for sub in range(2):
            for flow in range(4):
                total = partial(flow, step, sub)
                if not first:
                    ring_copy(flow, step - 1, sub).wait_recv()
                    total += ring_recv[flow, step - 1, sub].astype(F32)
                ring_send[flow, step, sub] = total.astype(BF16)
                ring_copy(flow, step, sub).start()

    ring_step(0, True)

    @pl.loop(0, KV_HEADS)
    def _(g):
        columns = pl.ds(pl.multiple_of(g * HEAD, HEAD), HEAD)
        values = v_ref[:, columns]
        total = jnp.zeros((BLOCK, HEAD), F32)
        for pair in range(GROUP // 2):
            first = g * GROUP * HEAD + pair * 2 * HEAD
            prob_grads = nt_dot(values, stacked(g_ref, first))
            probs = probs_buf[g * (GROUP // 2) + pair]
            row_dots = jnp.sum(
                probs.astype(BF16).astype(F32) * prob_grads, axis=0, keepdims=True
            )
            score_grads = (probs * (prob_grads - row_dots)).astype(BF16)
            total += jnp.dot(score_grads, stacked(q_ref, first), preferred_element_type=F32)
        key_ref[:, columns] = (total * factor).astype(BF16)

    @pl.loop(1, RING - 1)
    def _(step):
        ring_step(step, False)

    last = RING - 1
    for sub in range(2):
        for flow in range(4):
            total = partial(flow, last, sub)
            ring_copy(flow, last - 1, sub).wait_recv()
            total = (total + ring_recv[flow, last - 1, sub].astype(F32)).astype(BF16)
            for i in range(4):
                piece = total[:, i * BLOCK : (i + 1) * BLOCK]
                if FLOWS[flow][0] == "y":
                    zx_send[sub * NZL + i, flow] = piece
                else:
                    yx_send[4 * sub + i, flow - 2] = piece

    def zx_copy(to, slot, i):
        return pltpu.make_async_remote_copy(
            src_ref=zx_send.at[to], dst_ref=zx_recv.at[slot],
            send_sem=zx_ssem.at[i], recv_sem=zx_rsem.at[slot],
            device_id=device(x, y, to, c), device_id_type=MESH,
        )

    def yx_copy(to, slot, i):
        return pltpu.make_async_remote_copy(
            src_ref=yx_send.at[to], dst_ref=yx_recv.at[slot],
            send_sem=yx_ssem.at[i], recv_sem=yx_rsem.at[slot],
            device_id=device(x, to, z, c), device_id_type=MESH,
        )

    for i in range(1, RING):
        zx_copy(wrap(z + i, NZ), z, i).start()
        yx_copy(wrap(y + i, NY), y, i).start()
    zx_recv[z] = zx_send[z]
    yx_recv[y] = yx_send[y]
    for i in range(1, RING):
        zx_copy(wrap(z + i, NZ), wrap(z - i, NZ), i).wait_recv()
        yx_copy(wrap(y + i, NY), wrap(y - i, NY), i).wait_recv()
    zx_total = zx_recv[0].astype(F32)
    yx_total = yx_recv[0].astype(F32)
    for i in range(1, RING):
        zx_total += zx_recv[i].astype(F32)
        yx_total += yx_recv[i].astype(F32)
    x_send[0:2] = zx_total.astype(BF16)
    x_send[2:4] = yx_total.astype(BF16)

    def x_copy(to, slot, i):
        return pltpu.make_async_remote_copy(
            src_ref=x_send.at[to], dst_ref=x_recv.at[slot],
            send_sem=x_ssem.at[i], recv_sem=x_rsem.at[slot],
            device_id=device(to, y, z, c), device_id_type=MESH,
        )

    for i in range(1, NX):
        x_copy(wrap(x + i, NX), x, i).start()
    x_recv[x] = x_send[x]
    for i in range(1, NX):
        x_copy(wrap(x + i, NX), wrap(x - i, NX), i).wait_recv()
    final = x_recv[0].astype(F32)
    for i in range(1, NX):
        final += x_recv[i].astype(F32)
    final = final * (1.0 / math.sqrt(BLOCK * f_count * NX * CORES * (NZ // NZL)))

    def gather_copy(from_x, from_zh, to_x, to_zh, i, slot):
        rows = pl.ds(pl.multiple_of(from_x * HEAD + from_zh * HALF, HALF), HALF)
        return pltpu.make_async_remote_copy(
            src_ref=window.at[1 + c, rows], dst_ref=window.at[1 + c, rows],
            send_sem=gather_ssem.at[i], recv_sem=gather_rsem.at[slot],
            device_id=device(to_x, y, to_zh * NZL + zl, c), device_id_type=MESH,
        )

    own_rows = pl.ds(pl.multiple_of(x * HEAD + zh * HALF, HALF), HALF)
    window[1 + c, own_rows] = final.astype(BF16)
    moves = [(i, j) for j in (1, 0) for i in range(NX) if i or j]
    for n, (i, j) in enumerate(moves):
        to_x, to_zh = wrap(x + i, NX), wrap(zh + j, 2)
        gather_copy(x, zh, to_x, to_zh, n, zh * NX + x).start()
    for n, (i, j) in enumerate(moves):
        from_x, from_zh = wrap(x - i, NX), wrap(zh - j, 2)
        gather_copy(from_x, from_zh, x, zh, n, from_zh * NX + from_x).wait_recv()

    def spread_copy(block, slot, target):
        return pltpu.make_async_remote_copy(
            src_ref=window.at[1 + c], dst_ref=window.at[block],
            send_sem=spread_ssem.at[slot], recv_sem=spread_rsem.at[slot],
            device_id=target, device_id_type=MESH,
        )

    outer = 3 * (1 - c)

    def outer_copy(n, target):
        return pltpu.make_async_remote_copy(
            src_ref=window.at[1 + c], dst_ref=window.at[outer],
            send_sem=spread_ssem.at[1 + n], recv_sem=spread_rsem.at[1 + c],
            device_id=target, device_id_type=MESH,
        )

    outer_copy(0, (rep, far)).start()
    outer_copy(1, (rep + 1 - 2 * c, far)).start()
    spread_copy(1 + c, 0, sibling).start()

    def put(block):
        win_ref[block * BLOCK : (block + 1) * BLOCK, :] = window[block].astype(F32).T.astype(BF16)

    win_ref[4 * BLOCK :, :] = jnp.zeros((BLOCK, KV_HEADS * HEAD), BF16)
    pltpu.make_async_copy(window.at[2 - c], window.at[2 - c], spread_rsem.at[0]).wait()
    put(1)
    put(2)
    for n, block in ((0, 3), (1, 0)):
        pltpu.make_async_copy(window.at[block], window.at[block], spread_rsem.at[1 + n]).wait()
        put(block)

    pltpu.make_async_copy(far_half, far_half, acts_sems.at[0]).wait()
    vg_copy.wait_send()

    @pl.loop(0, RING - 1)
    def _(step):
        for flow in range(4):
            for sub in range(2):
                ring_copy(flow, step, sub).wait_send()

    for i in range(1, RING):
        zx_copy(wrap(z + i, NZ), z, i).wait_send()
        yx_copy(wrap(y + i, NY), y, i).wait_send()
    for i in range(1, NX):
        x_copy(wrap(x + i, NX), x, i).wait_send()
    for n, (i, j) in enumerate(moves):
        gather_copy(x, zh, wrap(x + i, NX), wrap(zh + j, 2), n, zh * NX + x).wait_send()
    outer_copy(0, (rep, far)).wait_send()
    outer_copy(1, (rep + 1 - 2 * c, far)).wait_send()
    spread_copy(1 + c, 0, sibling).wait_send()


def backward(activations, queries, keys, values, out_grad, positions):
    width = KV_HEADS * HEAD
    vmem = pl.BlockSpec(memory_space=pltpu.VMEM)
    dma = pltpu.SemaphoreType.DMA
    ring = (4, RING - 1, 2)
    return pl.pallas_call(
        kernel,
        out_shape=(
            jax.ShapeDtypeStruct((BLOCK, width), BF16),
            jax.ShapeDtypeStruct((5 * BLOCK, width), BF16),
        ),
        in_specs=[vmem] * 5 + [pl.BlockSpec(memory_space=pl.ANY)],
        out_specs=(vmem, vmem),
        scratch_shapes=[
            pltpu.VMEM((NY * NZL, 2 * BLOCK, BLOCK), BF16),
            pltpu.VMEM((width, 2 * BLOCK), BF16),
            pltpu.VMEM((KV_HEADS * GROUP // 2, BLOCK, 2 * BLOCK), F32),
            pltpu.VMEM(ring + (HALF, 4 * BLOCK), BF16),
            pltpu.VMEM(ring + (HALF, 4 * BLOCK), BF16),
            pltpu.VMEM((NZ, 2, HALF, BLOCK), BF16),
            pltpu.VMEM((NZ, 2, HALF, BLOCK), BF16),
            pltpu.VMEM((NY, 2, HALF, BLOCK), BF16),
            pltpu.VMEM((NY, 2, HALF, BLOCK), BF16),
            pltpu.VMEM((NX, HALF, BLOCK), BF16),
            pltpu.VMEM((NX, HALF, BLOCK), BF16),
            pltpu.VMEM((4, width, BLOCK), BF16),
            dma((1,)), dma((2,)), dma((2,)), dma(ring), dma(ring),
            dma((RING,)), dma((RING,)), dma((RING,)), dma((RING,)), dma((NX,)), dma((NX,)),
            dma((RING,)), dma((RING,)), dma((3,)), dma((3,)),
        ],
        compiler_params=pltpu.CompilerParams(
            collective_id=0, has_side_effects=True, vmem_limit_bytes=48 * 1024 * 1024
        ),
        cost_estimate=pl.CostEstimate(
            flops=2 * 10**9, bytes_accessed=6 * 2**20, transcendentals=2**19
        ),
    )(queries, keys, values, out_grad, positions.reshape(1, BLOCK), activations)


def shards(activations, queries, keys, values, out_grad, positions, shard_table):
    key_grad, window = backward(activations, queries, keys, values, out_grad, positions)
    stride = activations.shape[1] // lax.axis_size("fsdp")
    margin = stride // 2
    slot_rows = stride + stride // 4
    device_index = lax.axis_index("fsdp")
    offset = shard_table[0, 0, 0]
    length = shard_table[0, 0, 1]
    first_row = offset - (device_index * stride - margin)
    picked = lax.dynamic_slice_in_dim(window, first_row, slot_rows, 0)
    inside = jnp.arange(slot_rows, dtype=jnp.int32) < length
    slot_grad = jnp.where(inside[:, None], picked, jnp.zeros((), BF16))
    return (key_grad, slot_grad.reshape(1, 1, slot_rows, slot_grad.shape[1]))


def solution(mesh):
    return jax.shard_map(
        shards,
        mesh=mesh,
        in_specs=(
            P(("rep", "fsdp"), None),
            P(("rep", "fsdp"), None),
            P(("rep", "fsdp"), None),
            P(("rep", "fsdp"), None),
            P(("rep", "fsdp"), None),
            P(("rep", "fsdp")),
            P("rep", "fsdp", None),
        ),
        out_specs=(P(("rep", "fsdp"), None), P("rep", "fsdp", None, None)),
        check_vma=False,
    )
```

time: 478 us -> 88.6 us (0.19)
  waiting for transfers between devices: 409 us -> 0 us
  Pallas kernels: 0 us -> 76.3 us
  matrix products: 14.6 us -> 0 us
  starting transfers between devices: 13.8 us -> 0 us
  between operations: 14.9 us -> 1.32 us
  local copies, waits for them, and re-layouts: 17.7 us -> 8.47 us
  other arithmetic: 6.92 us -> 1.51 us
    psum x1 -> x0, waiting for transfers between devices: 201 us -> none  [shards(): window = lax.psum(partial_value, 'rep')]
    all_gather x1 -> x0, waiting for transfers between devices: 111 us -> none  [shards(): lax.all_gather(value_grad, 'fsdp', axis=0, tiled=True)]
    all_to_all x1 -> x0, waiting for transfers between devices: 97.1 us -> none  [shards(): lax.all_to_all(spans, 'fsdp', split_axis=1, concat_axis=0, tiled=True)]
    pallas_call x0 -> x1, Pallas kernels: none -> 76.3 us  [backward(): pl.pallas_call(kernel, out_shape=(jax.ShapeDtypeStruct((BLOCK, width), BF...]
    all_to_all x1 -> x0, starting transfers between devices: 13.7 us -> none  [shards(): lax.all_to_all(spans, 'fsdp', split_axis=1, concat_axis=0, tiled=True)]
    dot_general x4 -> x0, matrix products: 12.4 us -> none  [the longest x1 6.81 us: accumulate_with(): lax.dot_general(columns, incoming, (((0,), (0,)), ((), ())), preferred_el...]
    all_to_all x1 -> x0, local copies, waits for them, and re-layouts: 6.49 us -> none  [shards(): lax.all_to_all(spans, 'fsdp', split_axis=1, concat_axis=0, tiled=True)]
  transfers between devices with their start and end apart: 3 -> 0, of which waited for: 3 -> 0; matrix products, arithmetic and copies ran while one was open for 5% -> 0% of each run, Pallas kernels for 0% -> 0%
where the time goes in v1:
time: 88.6 us; the launch traced here: 87.6 us
  Pallas kernels  76.3 us (86%)
  local copies, waits for them, and re-layouts  8.47 us (10%)
  other arithmetic  1.51 us (2%)
  between operations  1.32 us (1%)
    pallas_call x1, Pallas kernels, backward(): pl.pallas_call(kernel, out_shape=(jax.ShapeDtypeStruct((BLOCK, width), BF...  76.3 us
    unnamed x13, local copies, waits for them, and re-layouts  7.15 us

profile of v1, /device:TPU:1, one launch (start us, length us, event | category | flops | bytes accessed | tf_op | source)
XLA Modules:
  0.0 87.6 jit_solution(5255136596715189400)
XLA Ops:
  0.6 1.3 %fusion = (s32[1,1,1]{2,1,0:T(1,128)}, s32[1,1,1]{2,1,0:T(1,128)}) fusion(s32[1,1,2]{2,1,0:T(1,128)} %param.13), kind=kLoop, calls=%fused_computation.2 | loop fusion | bytes 16 | tf_op jit(solution)/shard_map/slice | solution.py:385
  2.6 0.7 iota_compare_fusion
  3.3 0.0 copy-start
  3.3 1.6 %copy-done = bf16[128,8192]{1,0:T(8,128)(2,1)S(1)} copy-done((bf16[128,8192]{1,0:T(8,128)(2,1)S(1)}, bf16[128,8192]{1,0:T(8,128)(2,1)}, u32[]{:S(2)}) %copy-start) | copy-done | bytes 2097176
  4.9 0.0 copy-start.1
  4.9 1.2 %copy-done.1 = bf16[128,4096]{1,0:T(8,128)(2,1)S(1)} copy-done((bf16[128,4096]{1,0:T(8,128)(2,1)S(1)}, bf16[128,4096]{1,0:T(8,128)(2,1)}, u32[]{:S(2)}) %copy-start.1) | copy-done | bytes 1048600
  6.1 0.0 copy-start.2
  6.1 1.2 %copy-done.2 = bf16[128,4096]{1,0:T(8,128)(2,1)S(1)} copy-done((bf16[128,4096]{1,0:T(8,128)(2,1)S(1)}, bf16[128,4096]{1,0:T(8,128)(2,1)}, u32[]{:S(2)}) %copy-start.2) | copy-done | bytes 1048600
  7.3 0.0 copy-start.3
  7.3 0.9 %copy-done.3 = bf16[128,512]{1,0:T(8,128)(2,1)S(1)} copy-done((bf16[128,512]{1,0:T(8,128)(2,1)S(1)}, bf16[128,512]{1,0:T(8,128)(2,1)}, u32[]{:S(2)}) %copy-start.3) | copy-done | bytes 131096
  8.2 0.0 copy-start.4
  8.2 0.9 %copy-done.4 = bf16[128,512]{1,0:T(8,128)(2,1)S(1)} copy-done((bf16[128,512]{1,0:T(8,128)(2,1)S(1)}, bf16[128,512]{1,0:T(8,128)(2,1)}, u32[]{:S(2)}) %copy-start.4) | copy-done | bytes 131096
  9.1 0.0 copy-start.5
  9.1 0.7 copy-done.5
  9.8 76.3 %shard_map.86 = (bf16[128,512]{1,0:T(8,128)(2,1)S(1)}, bf16[640,512]{1,0:T(8,128)(2,1)S(1)}) custom-call(bf16[128,4096]{1,0:T(8,128)(2,1)S(1)} %copy-done.1, bf16[128,512]{1,0:T(8,128)(2,1)S(1)} %copy-done.3, bf16[128,512]{1,0:T(8,128)(2,1)S(1)} %copy-done.4, bf16[128,4096]{1,0:T(8,128)(2,1)S(1)} %copy-done.2, s32[1,128]{1,0:T(1,128)S(1)} %bitcast.5, ...), custom_call_target="tpu_custom_call" | custom-call | flops 2000000000 | bytes 6291456 | tf_op jit(solution)/shard_map/pallas_call | solution.py:344
  86.1 0.9 select_bitcast_fusion
  86.9 0.7 copy.10
Async XLA Ops:
  3.3 1.6 %copy-start = (bf16[128,8192]{1,0:T(8,128)(2,1)S(1)}, bf16[128,8192]{1,0:T(8,128)(2,1)}, u32[]{:S(2)}) copy-start(bf16[128,8192]{1,0:T(8,128)(2,1)} %acts_ref.1) | copy-start | bytes 6291460
  4.9 1.2 %copy-start.1 = (bf16[128,4096]{1,0:T(8,128)(2,1)S(1)}, bf16[128,4096]{1,0:T(8,128)(2,1)}, u32[]{:S(2)}) copy-start(bf16[128,4096]{1,0:T(8,128)(2,1)} %q_ref.1) | copy-start | bytes 3145732
  6.1 1.2 %copy-start.2 = (bf16[128,4096]{1,0:T(8,128)(2,1)S(1)}, bf16[128,4096]{1,0:T(8,128)(2,1)}, u32[]{:S(2)}) copy-start(bf16[128,4096]{1,0:T(8,128)(2,1)} %g_ref.1) | copy-start | bytes 3145732
  7.3 0.9 %copy-start.3 = (bf16[128,512]{1,0:T(8,128)(2,1)S(1)}, bf16[128,512]{1,0:T(8,128)(2,1)}, u32[]{:S(2)}) copy-start(bf16[128,512]{1,0:T(8,128)(2,1)} %k_ref.1) | copy-start | bytes 393220
  8.2 0.9 %copy-start.4 = (bf16[128,512]{1,0:T(8,128)(2,1)S(1)}, bf16[128,512]{1,0:T(8,128)(2,1)}, u32[]{:S(2)}) copy-start(bf16[128,512]{1,0:T(8,128)(2,1)} %v_ref.1) | copy-start | bytes 393220
  9.1 0.7 copy-start.5

commit v2 on v1

--- a/solution.py
+++ b/solution.py
@@ -33,11 +33,11 @@
 
 
 def kernel(
-    q_ref, k_ref, v_ref, g_ref, pos_ref, acts_ref,
-    key_ref, win_ref,
-    acts_buf, vgt_buf, probs_buf, ring_send, ring_recv,
+    table_ref, pos_ref, q_hbm, k_hbm, v_hbm, g_hbm, acts_ref,
+    key_ref, slot_ref,
+    q_ref, k_ref, v_ref, g_ref, acts_buf, vgt_buf, probs_buf, ring_send, ring_recv,
     zx_send, zx_recv, yx_send, yx_recv, x_send, x_recv, window,
-    local_sem, acts_sems, vg_sems, ring_ssem, ring_rsem,
+    load_sems, local_sem, acts_sems, vg_sems, ring_ssem, ring_rsem,
     zx_ssem, zx_rsem, yx_ssem, yx_rsem, x_ssem, x_rsem,
     gather_ssem, gather_rsem, spread_ssem, spread_rsem,
 ):
@@ -51,6 +51,23 @@
     f_count = NY * NZL
     far = lax.rem(fsdp + f_count - 1 + 2 * c, f_count)
     far_other = lax.rem(fsdp + f_count + 1 - 2 * c, f_count)
+
+    heads = KV_HEADS * HEAD
+    span = GROUP * HEAD
+
+    def load(n, source, target, first, size):
+        part = pl.ds(first, size)
+        return pltpu.make_async_copy(source.at[:, part], target.at[:, part], load_sems.at[n])
+
+    load_keys = load(0, k_hbm, k_ref, 0, heads)
+    load_values = load(1, v_hbm, v_ref, 0, heads)
+    load_queries = [load(2 + g, q_hbm, q_ref, g * span, span) for g in range(KV_HEADS)]
+    load_grads = [load(6 + g, g_hbm, g_ref, g * span, span) for g in range(KV_HEADS)]
+    load_keys.start()
+    for g in range(KV_HEADS):
+        load_queries[g].start()
+        load_grads[g].start()
+    load_values.start()
 
     partners = [sibling]
     partners += [device(x, wrap(y + i, NY), z, c) for i in range(1, NY)]
@@ -112,6 +129,11 @@
             )
         vgt_buf[pl.ds(pl.multiple_of(g * HEAD, HEAD), HEAD), pl.ds(0, BLOCK)] = total.T.astype(BF16)
 
+    load_keys.wait()
+    for g in range(2):
+        load_queries[g].wait()
+        load_grads[g].wait()
+
     @pl.loop(0, 2)
     def _(g):
         values_of(g)
@@ -121,6 +143,10 @@
     @pl.loop(0, f_count)
     def _(f):
         send_acts(f).start()
+
+    for g in range(2, KV_HEADS):
+        load_queries[g].wait()
+        load_grads[g].wait()
 
     @pl.loop(2, KV_HEADS)
     def _(g):
@@ -185,6 +211,8 @@
                 ring_copy(flow, step, sub).start()
 
     ring_step(0, True)
+
+    load_values.wait()
 
     @pl.loop(0, KV_HEADS)
     def _(g):
@@ -304,16 +332,18 @@
     outer_copy(1, (rep + 1 - 2 * c, far)).start()
     spread_copy(1 + c, 0, sibling).start()
 
-    def put(block):
-        win_ref[block * BLOCK : (block + 1) * BLOCK, :] = window[block].astype(F32).T.astype(BF16)
-
-    win_ref[4 * BLOCK :, :] = jnp.zeros((BLOCK, KV_HEADS * HEAD), BF16)
     pltpu.make_async_copy(window.at[2 - c], window.at[2 - c], spread_rsem.at[0]).wait()
-    put(1)
-    put(2)
-    for n, block in ((0, 3), (1, 0)):
-        pltpu.make_async_copy(window.at[block], window.at[block], spread_rsem.at[1 + n]).wait()
-        put(block)
+    pltpu.make_async_copy(window.at[3], window.at[3], spread_rsem.at[1]).wait()
+    pltpu.make_async_copy(window.at[0], window.at[0], spread_rsem.at[2]).wait()
+    first_row = table_ref[0, 0] - (2 * BLOCK * fsdp - BLOCK)
+    columns = jnp.concatenate([window[block] for block in range(4)], axis=1)
+    for start in range(0, slot_ref.shape[0], HALF):
+        row = start + lax.broadcasted_iota(jnp.int32, (HALF, 4 * BLOCK), 0)
+        source = lax.broadcasted_iota(jnp.int32, (HALF, 4 * BLOCK), 1)
+        chosen = (source == row + first_row) & (row < table_ref[0, 1])
+        slot_ref[start : start + HALF, :] = nt_dot(
+            jnp.where(chosen, 1.0, 0.0).astype(BF16), columns
+        ).astype(BF16)
 
     pltpu.make_async_copy(far_half, far_half, acts_sems.at[0]).wait()
     vg_copy.wait_send()
@@ -336,20 +366,27 @@
     spread_copy(1 + c, 0, sibling).wait_send()
 
 
-def backward(activations, queries, keys, values, out_grad, positions):
-    width = KV_HEADS * HEAD
+def shards(activations, queries, keys, values, out_grad, positions, shard_table):
+    tokens, width = keys.shape
+    stride = activations.shape[1] // lax.axis_size("fsdp")
+    slot_rows = stride + stride // 4
     vmem = pl.BlockSpec(memory_space=pltpu.VMEM)
+    hbm = pl.BlockSpec(memory_space=pltpu.HBM)
     dma = pltpu.SemaphoreType.DMA
     ring = (4, RING - 1, 2)
-    return pl.pallas_call(
+    key_grad, slot_grad = pl.pallas_call(
         kernel,
         out_shape=(
-            jax.ShapeDtypeStruct((BLOCK, width), BF16),
-            jax.ShapeDtypeStruct((5 * BLOCK, width), BF16),
+            jax.ShapeDtypeStruct((tokens, width), BF16),
+            jax.ShapeDtypeStruct((slot_rows, width), BF16),
         ),
-        in_specs=[vmem] * 5 + [pl.BlockSpec(memory_space=pl.ANY)],
+        in_specs=[pl.BlockSpec(memory_space=pltpu.SMEM), vmem] + [hbm] * 5,
         out_specs=(vmem, vmem),
         scratch_shapes=[
+            pltpu.VMEM(queries.shape, BF16),
+            pltpu.VMEM(keys.shape, BF16),
+            pltpu.VMEM(values.shape, BF16),
+            pltpu.VMEM(out_grad.shape, BF16),
             pltpu.VMEM((NY * NZL, 2 * BLOCK, BLOCK), BF16),
             pltpu.VMEM((width, 2 * BLOCK), BF16),
             pltpu.VMEM((KV_HEADS * GROUP // 2, BLOCK, 2 * BLOCK), F32),
@@ -362,32 +399,21 @@
             pltpu.VMEM((NX, HALF, BLOCK), BF16),
             pltpu.VMEM((NX, HALF, BLOCK), BF16),
             pltpu.VMEM((4, width, BLOCK), BF16),
-            dma((1,)), dma((2,)), dma((2,)), dma(ring), dma(ring),
+            dma((10,)), dma((1,)), dma((2,)), dma((2,)), dma(ring), dma(ring),
             dma((RING,)), dma((RING,)), dma((RING,)), dma((RING,)), dma((NX,)), dma((NX,)),
             dma((RING,)), dma((RING,)), dma((3,)), dma((3,)),
         ],
         compiler_params=pltpu.CompilerParams(
-            collective_id=0, has_side_effects=True, vmem_limit_bytes=48 * 1024 * 1024
+            collective_id=0, has_side_effects=True, vmem_limit_bytes=62 * 1024 * 1024
         ),
         cost_estimate=pl.CostEstimate(
             flops=2 * 10**9, bytes_accessed=6 * 2**20, transcendentals=2**19
         ),
-    )(queries, keys, values, out_grad, positions.reshape(1, BLOCK), activations)
-
-
-def shards(activations, queries, keys, values, out_grad, positions, shard_table):
-    key_grad, window = backward(activations, queries, keys, values, out_grad, positions)
-    stride = activations.shape[1] // lax.axis_size("fsdp")
-    margin = stride // 2
-    slot_rows = stride + stride // 4
-    device_index = lax.axis_index("fsdp")
-    offset = shard_table[0, 0, 0]
-    length = shard_table[0, 0, 1]
-    first_row = offset - (device_index * stride - margin)
-    picked = lax.dynamic_slice_in_dim(window, first_row, slot_rows, 0)
-    inside = jnp.arange(slot_rows, dtype=jnp.int32) < length
-    slot_grad = jnp.where(inside[:, None], picked, jnp.zeros((), BF16))
-    return (key_grad, slot_grad.reshape(1, 1, slot_rows, slot_grad.shape[1]))
+    )(
+        shard_table.reshape(1, 2), positions.reshape(1, tokens),
+        queries, keys, values, out_grad, activations,
+    )
+    return (key_grad, slot_grad.reshape(1, 1, slot_rows, width))
 
 
 def solution(mesh):

time: 88.6 us -> 83.3 us (0.940)
  local copies, waits for them, and re-layouts: 8.47 us -> 3.29 us
  Pallas kernels: 76.3 us -> 78.6 us
  other arithmetic: 1.51 us -> 0 us
    unnamed x13 -> x2, local copies, waits for them, and re-layouts: 7.15 us -> 3.29 us
    pallas_call x1, Pallas kernels: 76.3 us -> 78.6 us  [shards(): pl.pallas_call(kernel, out_shape=(jax.ShapeDtypeStruct((tokens, width), B...]
    slice x1 -> x0, local copies, waits for them, and re-layouts: 1.31 us -> none  [shards(): length = shard_table[0, 0, 1]]
where the time goes in v2:
time: 83.3 us; the launch traced here: 82.5 us
  Pallas kernels  78.6 us (94%)
  local copies, waits for them, and re-layouts  3.29 us (4%)
    pallas_call x1, Pallas kernels, shards(): pl.pallas_call(kernel, out_shape=(jax.ShapeDtypeStruct((tokens, width), B...  78.6 us
    unnamed x2, local copies, waits for them, and re-layouts  3.29 us

profile of v2, /device:TPU:1, one launch (start us, length us, event | category | flops | bytes accessed | tf_op | source)
XLA Modules:
  0.0 82.5 jit_solution(16320355079949944185)
XLA Ops:
  0.6 78.6 %shard_map.86 = (bf16[128,512]{1,0:T(8,128)(2,1)}, bf16[320,512]{1,0:T(8,128)(2,1)}) custom-call(s32[1,2]{1,0:T(1,128)} %bitcast.4, s32[1,128]{1,0:T(1,128)} %bitcast.5, bf16[128,4096]{1,0:T(8,128)(2,1)} %q_hbm.1, bf16[128,512]{1,0:T(8,128)(2,1)} %k_hbm.1, bf16[128,512]{1,0:T(8,128)(2,1)} %v_hbm.1, bf16[128,4096]{1,0:T(8,128)(2,1)} %g_hbm.1, ...), custom_call_target="tpu_custom_call" | custom-call | flops 2000000000 | bytes 6291456 | tf_op jit(solution)/shard_map/pallas_call | solution.py:377
  79.3 1.6 %copy.11 = bf16[128,512]{1,0:T(8,128)(2,1)} copy(bf16[128,512]{1,0:T(8,128)(2,1)} %get-tuple-element.8) | data formatting | bytes 262144
  80.8 1.7 %copy.12 = bf16[1,1,320,512]{3,2,1,0:T(8,128)(2,1)} copy(bf16[1,1,320,512]{3,2,1,0:T(8,128)(2,1)} %bitcast.3) | data formatting | bytes 655360

commit v3 on v2

--- a/solution.py
+++ b/solution.py
@@ -16,7 +16,11 @@
 HALF = 64
 BF16, F32 = jnp.bfloat16, jnp.float32
 MESH = pl.DeviceIdType.MESH
-FLOWS = (("y", 1, 0), ("y", -1, 1), ("z", 1, 2), ("z", -1, 3))
+AXES = ("y", "y", "z", "z")
+HOPS = 4
+FLOWS = tuple((g, 1 - 2 * (g % 2), HOPS) for g in range(KV_HEADS)) + tuple(
+    (g, 2 * (g % 2) - 1, HOPS - 1) for g in range(KV_HEADS)
+)
 
 
 def device(x, y, z, c):
@@ -49,8 +53,10 @@
     z = zh * NZL + zl
     sibling = device(x, y, z, 1 - c)
     f_count = NY * NZL
-    far = lax.rem(fsdp + f_count - 1 + 2 * c, f_count)
-    far_other = lax.rem(fsdp + f_count + 1 - 2 * c, f_count)
+
+    def beside(way, core):
+        edge = jnp.where(zl == (NZL - 1 if way == 1 else 0), way, 0)
+        return device(x, wrap(y + edge, NY), wrap(z + way, NZ), core)
 
     heads = KV_HEADS * HEAD
     span = GROUP * HEAD
@@ -74,8 +80,7 @@
     partners += [device(x, y, wrap(z + i, NZ), c) for i in range(1, NZ)]
     partners += [device(wrap(x + i, NX), y, z, c) for i in range(1, NX)]
     partners += [device(wrap(x + i, NX), y, wrap(z + NZL, NZ), c) for i in range(1, NX)]
-    for other in (far, far_other):
-        partners += [(rep, other), (rep + 1 - 2 * c, other)]
+    partners += [beside(way, core) for way in (1, -1) for core in (0, 1)]
     barrier = pltpu.get_barrier_semaphore()
     for partner in partners:
         pl.semaphore_signal(barrier, inc=1, device_id=partner, device_id_type=MESH)
@@ -171,8 +176,8 @@
         return y if axis == "y" else z
 
     def ring_copy(flow, step, sub):
-        axis, way, _ = FLOWS[flow]
-        if axis == "y":
+        g, way, _ = FLOWS[flow]
+        if AXES[g] == "y":
             target = device(x, wrap(y + way, NY), z, c)
         else:
             target = device(x, y, wrap(z + way, NZ), c)
@@ -185,10 +190,9 @@
             device_id_type=MESH,
         )
 
-    def partial(flow, step, sub):
-        axis, way, g = FLOWS[flow]
-        chunk = wrap(place(axis) - way * (1 + step), RING)
-        if axis == "y":
+    def partial(g, distance, sub):
+        chunk = wrap(place(AXES[g]) + distance, RING)
+        if AXES[g] == "y":
             columns = g * HEAD + sub * HALF
             blocks = [acts_buf[chunk * NZL + i] for i in range(4)]
         else:
@@ -200,17 +204,19 @@
             preferred_element_type=F32,
         )
 
-    def ring_step(step, first):
-        for sub in range(2):
-            for flow in range(4):
-                total = partial(flow, step, sub)
-                if not first:
-                    ring_copy(flow, step - 1, sub).wait_recv()
-                    total += ring_recv[flow, step - 1, sub].astype(F32)
-                ring_send[flow, step, sub] = total.astype(BF16)
-                ring_copy(flow, step, sub).start()
-
-    ring_step(0, True)
+    def ring_step(step, flows, first=False):
+        for half in range(0, flows, KV_HEADS):
+            for sub in range(2):
+                for flow in range(half, half + KV_HEADS):
+                    g, way, hops = FLOWS[flow]
+                    total = partial(g, way * (hops - step), sub)
+                    if not first:
+                        ring_copy(flow, step - 1, sub).wait_recv()
+                        total += ring_recv[flow, step - 1, sub].astype(F32)
+                    ring_send[flow, step, sub] = total.astype(BF16)
+                    ring_copy(flow, step, sub).start()
+
+    ring_step(0, 2 * KV_HEADS, True)
 
     load_values.wait()
 
@@ -230,22 +236,25 @@
             total += jnp.dot(score_grads, stacked(q_ref, first), preferred_element_type=F32)
         key_ref[:, columns] = (total * factor).astype(BF16)
 
-    @pl.loop(1, RING - 1)
+    @pl.loop(1, HOPS - 1)
     def _(step):
-        ring_step(step, False)
-
-    last = RING - 1
+        ring_step(step, 2 * KV_HEADS)
+
+    ring_step(HOPS - 1, KV_HEADS)
     for sub in range(2):
-        for flow in range(4):
-            total = partial(flow, last, sub)
-            ring_copy(flow, last - 1, sub).wait_recv()
-            total = (total + ring_recv[flow, last - 1, sub].astype(F32)).astype(BF16)
+        for g in range(KV_HEADS):
+            total = partial(g, 0, sub)
+            for flow in (g + KV_HEADS, g):
+                hops = FLOWS[flow][2]
+                ring_copy(flow, hops - 1, sub).wait_recv()
+                total += ring_recv[flow, hops - 1, sub].astype(F32)
+            total = total.astype(BF16)
             for i in range(4):
                 piece = total[:, i * BLOCK : (i + 1) * BLOCK]
-                if FLOWS[flow][0] == "y":
-                    zx_send[sub * NZL + i, flow] = piece
+                if AXES[g] == "y":
+                    zx_send[sub * NZL + i, g] = piece
                 else:
-                    yx_send[4 * sub + i, flow - 2] = piece
+                    yx_send[4 * sub + i, g - 2] = piece
 
     def zx_copy(to, slot, i):
         return pltpu.make_async_remote_copy(
@@ -328,9 +337,26 @@
             device_id=target, device_id_type=MESH,
         )
 
-    outer_copy(0, (rep, far)).start()
-    outer_copy(1, (rep + 1 - 2 * c, far)).start()
+    before = [beside(-1, core) for core in (0, 1)]
+    after = [beside(1, core) for core in (0, 1)]
+    targets = [tuple(jnp.where(c == 0, a, b) for a, b in zip(before[n], after[n])) for n in (0, 1)]
+    outer_copy(0, targets[0]).start()
+    outer_copy(1, targets[1]).start()
     spread_copy(1 + c, 0, sibling).start()
+
+    pltpu.make_async_copy(far_half, far_half, acts_sems.at[0]).wait()
+    vg_copy.wait_send()
+    for flow in range(2 * KV_HEADS):
+        for step in range(FLOWS[flow][2]):
+            for sub in range(2):
+                ring_copy(flow, step, sub).wait_send()
+    for i in range(1, RING):
+        zx_copy(wrap(z + i, NZ), z, i).wait_send()
+        yx_copy(wrap(y + i, NY), y, i).wait_send()
+    for i in range(1, NX):
+        x_copy(wrap(x + i, NX), x, i).wait_send()
+    for n, (i, j) in enumerate(moves):
+        gather_copy(x, zh, wrap(x + i, NX), wrap(zh + j, 2), n, zh * NX + x).wait_send()
 
     pltpu.make_async_copy(window.at[2 - c], window.at[2 - c], spread_rsem.at[0]).wait()
     pltpu.make_async_copy(window.at[3], window.at[3], spread_rsem.at[1]).wait()
@@ -345,24 +371,8 @@
             jnp.where(chosen, 1.0, 0.0).astype(BF16), columns
         ).astype(BF16)
 
-    pltpu.make_async_copy(far_half, far_half, acts_sems.at[0]).wait()
-    vg_copy.wait_send()
-
-    @pl.loop(0, RING - 1)
-    def _(step):
-        for flow in range(4):
-            for sub in range(2):
-                ring_copy(flow, step, sub).wait_send()
-
-    for i in range(1, RING):
-        zx_copy(wrap(z + i, NZ), z, i).wait_send()
-        yx_copy(wrap(y + i, NY), y, i).wait_send()
-    for i in range(1, NX):
-        x_copy(wrap(x + i, NX), x, i).wait_send()
-    for n, (i, j) in enumerate(moves):
-        gather_copy(x, zh, wrap(x + i, NX), wrap(zh + j, 2), n, zh * NX + x).wait_send()
-    outer_copy(0, (rep, far)).wait_send()
-    outer_copy(1, (rep + 1 - 2 * c, far)).wait_send()
+    outer_copy(0, targets[0]).wait_send()
+    outer_copy(1, targets[1]).wait_send()
     spread_copy(1 + c, 0, sibling).wait_send()
 
 
@@ -373,12 +383,12 @@
     vmem = pl.BlockSpec(memory_space=pltpu.VMEM)
     hbm = pl.BlockSpec(memory_space=pltpu.HBM)
     dma = pltpu.SemaphoreType.DMA
-    ring = (4, RING - 1, 2)
+    ring = (2 * KV_HEADS, HOPS, 2)
     key_grad, slot_grad = pl.pallas_call(
         kernel,
         out_shape=(
-            jax.ShapeDtypeStruct((tokens, width), BF16),
-            jax.ShapeDtypeStruct((slot_rows, width), BF16),
+            pltpu.VMEM((tokens, width), BF16),
+            pltpu.VMEM((slot_rows, width), BF16),
         ),
         in_specs=[pl.BlockSpec(memory_space=pltpu.SMEM), vmem] + [hbm] * 5,
         out_specs=(vmem, vmem),

time: 83.3 us -> 72.5 us (0.87)
  Pallas kernels: 78.6 us -> 70.4 us
  local copies, waits for them, and re-layouts: 3.29 us -> 1.38 us
    pallas_call x1, Pallas kernels: 78.6 us -> 70.4 us  [shards(): pl.pallas_call(kernel, out_shape=(pltpu.VMEM((tokens, width), BF16), pltp...]
    unnamed x2, local copies, waits for them, and re-layouts: 3.29 us -> 1.38 us
where the time goes in v3:
time: 72.5 us; the launch traced here: 72.4 us
  Pallas kernels  70.4 us (97%)
  local copies, waits for them, and re-layouts  1.38 us (2%)
    pallas_call x1, Pallas kernels, shards(): pl.pallas_call(kernel, out_shape=(pltpu.VMEM((tokens, width), BF16), pltp...  70.4 us

profile of v3, /device:TPU:1, one launch (start us, length us, event | category | flops | bytes accessed | tf_op | source)
XLA Modules:
  0.0 72.4 jit_solution(4099914357381120606)
XLA Ops:
  0.6 70.4 %shard_map.86 = (bf16[128,512]{1,0:T(8,128)(2,1)S(1)}, bf16[320,512]{1,0:T(8,128)(2,1)S(1)}) custom-call(s32[1,2]{1,0:T(1,128)} %bitcast.4, s32[1,128]{1,0:T(1,128)} %bitcast.5, bf16[128,4096]{1,0:T(8,128)(2,1)} %q_hbm.1, bf16[128,512]{1,0:T(8,128)(2,1)} %k_hbm.1, bf16[128,512]{1,0:T(8,128)(2,1)} %v_hbm.1, bf16[128,4096]{1,0:T(8,128)(2,1)} %g_hbm.1, ...), custom_call_target="tpu_custom_call" | custom-call | flops 2000000000 | bytes 6291456 | tf_op jit(solution)/shard_map/pallas_call | solution.py:387
  71.0 0.7 copy.11
  71.7 0.7 copy.12

commit v4 on v3

--- a/solution.py
+++ b/solution.py
@@ -40,7 +40,7 @@
     table_ref, pos_ref, q_hbm, k_hbm, v_hbm, g_hbm, acts_ref,
     key_ref, slot_ref,
     q_ref, k_ref, v_ref, g_ref, acts_buf, vgt_buf, probs_buf, ring_send, ring_recv,
-    zx_send, zx_recv, yx_send, yx_recv, x_send, x_recv, window,
+    zx_send, zx_recv, yx_send, yx_recv, x_send, x_recv, window, chosen_buf, slot_buf,
     load_sems, local_sem, acts_sems, vg_sems, ring_ssem, ring_rsem,
     zx_ssem, zx_rsem, yx_ssem, yx_rsem, x_ssem, x_rsem,
     gather_ssem, gather_rsem, spread_ssem, spread_rsem,
@@ -76,11 +76,9 @@
     load_values.start()
 
     partners = [sibling]
-    partners += [device(x, wrap(y + i, NY), z, c) for i in range(1, NY)]
-    partners += [device(x, y, wrap(z + i, NZ), c) for i in range(1, NZ)]
+    partners += [device(x, wrap(y + i, NY), z, c) for i in (1, -1)]
+    partners += [device(x, y, wrap(z + i, NZ), c) for i in (1, -1)]
     partners += [device(wrap(x + i, NX), y, z, c) for i in range(1, NX)]
-    partners += [device(wrap(x + i, NX), y, wrap(z + NZL, NZ), c) for i in range(1, NX)]
-    partners += [beside(way, core) for way in (1, -1) for core in (0, 1)]
     barrier = pltpu.get_barrier_semaphore()
     for partner in partners:
         pl.semaphore_signal(barrier, inc=1, device_id=partner, device_id_type=MESH)
@@ -143,19 +141,19 @@
     def _(g):
         values_of(g)
 
+    for g in range(2, KV_HEADS):
+        load_queries[g].wait()
+        load_grads[g].wait()
+
+    @pl.loop(2, KV_HEADS)
+    def _(g):
+        values_of(g)
+
     pl.semaphore_wait(barrier, len(partners))
 
     @pl.loop(0, f_count)
     def _(f):
         send_acts(f).start()
-
-    for g in range(2, KV_HEADS):
-        load_queries[g].wait()
-        load_grads[g].wait()
-
-    @pl.loop(2, KV_HEADS)
-    def _(g):
-        values_of(g)
 
     vg_copy = pltpu.make_async_remote_copy(
         src_ref=vgt_buf.at[:, pl.ds(0, BLOCK)],
@@ -205,8 +203,8 @@
         )
 
     def ring_step(step, flows, first=False):
-        for half in range(0, flows, KV_HEADS):
-            for sub in range(2):
+        for sub in range(2):
+            for half in range(0, flows, KV_HEADS):
                 for flow in range(half, half + KV_HEADS):
                     g, way, hops = FLOWS[flow]
                     total = partial(g, way * (hops - step), sub)
@@ -217,6 +215,60 @@
                     ring_copy(flow, step, sub).start()
 
     ring_step(0, 2 * KV_HEADS, True)
+
+    @pl.loop(1, HOPS - 1)
+    def _(step):
+        ring_step(step, 2 * KV_HEADS)
+
+    def zx_copy(to, slot):
+        return pltpu.make_async_remote_copy(
+            src_ref=zx_send.at[to], dst_ref=zx_recv.at[slot],
+            send_sem=zx_ssem.at[to], recv_sem=zx_rsem.at[slot],
+            device_id=device(x, y, to, c), device_id_type=MESH,
+        )
+
+    def yx_copy(to, slot):
+        return pltpu.make_async_remote_copy(
+            src_ref=yx_send.at[to], dst_ref=yx_recv.at[slot],
+            send_sem=yx_ssem.at[to], recv_sem=yx_rsem.at[slot],
+            device_id=device(x, to, z, c), device_id_type=MESH,
+        )
+
+    ring_step(HOPS - 1, KV_HEADS)
+    for sub in range(2):
+        for g in range(KV_HEADS):
+            total = partial(g, 0, sub)
+            for flow in (g + KV_HEADS, g):
+                hops = FLOWS[flow][2]
+                ring_copy(flow, hops - 1, sub).wait_recv()
+                total += ring_recv[flow, hops - 1, sub].astype(F32)
+            total = total.astype(BF16)
+            for i in range(4):
+                piece = total[:, i * BLOCK : (i + 1) * BLOCK]
+                if AXES[g] == "y":
+                    zx_send[sub * NZL + i, g] = piece
+                else:
+                    yx_send[4 * sub + i, g - 2] = piece
+        for i in range(4):
+            to_z, to_y = 4 * sub + lax.rem(z + i, 4), 4 * sub + lax.rem(y + i, 4)
+
+            @pl.when(to_z != z)
+            def _():
+                zx_copy(to_z, z).start()
+
+            @pl.when(to_y != y)
+            def _():
+                yx_copy(to_y, y).start()
+
+    first_row = table_ref[0, 0] - (2 * BLOCK * fsdp - BLOCK)
+    for start in range(0, slot_ref.shape[0], HALF):
+        row = start + lax.broadcasted_iota(jnp.int32, (HALF, 4 * BLOCK), 0)
+        source = lax.broadcasted_iota(jnp.int32, (HALF, 4 * BLOCK), 1)
+        chosen = (source == row + first_row) & (row < table_ref[0, 1])
+        chosen_buf[pl.ds(start, HALF), :] = jnp.where(chosen, 1.0, 0.0).astype(BF16)
+
+    zx_recv[z] = zx_send[z]
+    yx_recv[y] = yx_send[y]
 
     load_values.wait()
 
@@ -236,48 +288,9 @@
             total += jnp.dot(score_grads, stacked(q_ref, first), preferred_element_type=F32)
         key_ref[:, columns] = (total * factor).astype(BF16)
 
-    @pl.loop(1, HOPS - 1)
-    def _(step):
-        ring_step(step, 2 * KV_HEADS)
-
-    ring_step(HOPS - 1, KV_HEADS)
-    for sub in range(2):
-        for g in range(KV_HEADS):
-            total = partial(g, 0, sub)
-            for flow in (g + KV_HEADS, g):
-                hops = FLOWS[flow][2]
-                ring_copy(flow, hops - 1, sub).wait_recv()
-                total += ring_recv[flow, hops - 1, sub].astype(F32)
-            total = total.astype(BF16)
-            for i in range(4):
-                piece = total[:, i * BLOCK : (i + 1) * BLOCK]
-                if AXES[g] == "y":
-                    zx_send[sub * NZL + i, g] = piece
-                else:
-                    yx_send[4 * sub + i, g - 2] = piece
-
-    def zx_copy(to, slot, i):
-        return pltpu.make_async_remote_copy(
-            src_ref=zx_send.at[to], dst_ref=zx_recv.at[slot],
-            send_sem=zx_ssem.at[i], recv_sem=zx_rsem.at[slot],
-            device_id=device(x, y, to, c), device_id_type=MESH,
-        )
-
-    def yx_copy(to, slot, i):
-        return pltpu.make_async_remote_copy(
-            src_ref=yx_send.at[to], dst_ref=yx_recv.at[slot],
-            send_sem=yx_ssem.at[i], recv_sem=yx_rsem.at[slot],
-            device_id=device(x, to, z, c), device_id_type=MESH,
-        )
-
     for i in range(1, RING):
-        zx_copy(wrap(z + i, NZ), z, i).start()
-        yx_copy(wrap(y + i, NY), y, i).start()
-    zx_recv[z] = zx_send[z]
-    yx_recv[y] = yx_send[y]
-    for i in range(1, RING):
-        zx_copy(wrap(z + i, NZ), wrap(z - i, NZ), i).wait_recv()
-        yx_copy(wrap(y + i, NY), wrap(y - i, NY), i).wait_recv()
+        zx_copy(wrap(z + i, NZ), wrap(z - i, NZ)).wait_recv()
+        yx_copy(wrap(y + i, NY), wrap(y - i, NY)).wait_recv()
     zx_total = zx_recv[0].astype(F32)
     yx_total = yx_recv[0].astype(F32)
     for i in range(1, RING):
@@ -304,45 +317,41 @@
     final = final * (1.0 / math.sqrt(BLOCK * f_count * NX * CORES * (NZ // NZL)))
 
     def gather_copy(from_x, from_zh, to_x, to_zh, i, slot):
-        rows = pl.ds(pl.multiple_of(from_x * HEAD + from_zh * HALF, HALF), HALF)
+        rows = pl.ds(pl.multiple_of((from_zh * NX + from_x) * HALF, HALF), HALF)
         return pltpu.make_async_remote_copy(
             src_ref=window.at[1 + c, rows], dst_ref=window.at[1 + c, rows],
             send_sem=gather_ssem.at[i], recv_sem=gather_rsem.at[slot],
             device_id=device(to_x, y, to_zh * NZL + zl, c), device_id_type=MESH,
         )
 
-    own_rows = pl.ds(pl.multiple_of(x * HEAD + zh * HALF, HALF), HALF)
+    own_rows = pl.ds(pl.multiple_of((zh * NX + x) * HALF, HALF), HALF)
     window[1 + c, own_rows] = final.astype(BF16)
     moves = [(i, j) for j in (1, 0) for i in range(NX) if i or j]
     for n, (i, j) in enumerate(moves):
         to_x, to_zh = wrap(x + i, NX), wrap(zh + j, 2)
         gather_copy(x, zh, to_x, to_zh, n, zh * NX + x).start()
-    for n, (i, j) in enumerate(moves):
-        from_x, from_zh = wrap(x - i, NX), wrap(zh - j, 2)
-        gather_copy(from_x, from_zh, x, zh, n, from_zh * NX + from_x).wait_recv()
-
-    def spread_copy(block, slot, target):
-        return pltpu.make_async_remote_copy(
-            src_ref=window.at[1 + c], dst_ref=window.at[block],
-            send_sem=spread_ssem.at[slot], recv_sem=spread_rsem.at[slot],
-            device_id=target, device_id_type=MESH,
-        )
-
-    outer = 3 * (1 - c)
-
-    def outer_copy(n, target):
-        return pltpu.make_async_remote_copy(
-            src_ref=window.at[1 + c], dst_ref=window.at[outer],
-            send_sem=spread_ssem.at[1 + n], recv_sem=spread_rsem.at[1 + c],
-            device_id=target, device_id_type=MESH,
-        )
-
     before = [beside(-1, core) for core in (0, 1)]
     after = [beside(1, core) for core in (0, 1)]
     targets = [tuple(jnp.where(c == 0, a, b) for a, b in zip(before[n], after[n])) for n in (0, 1)]
-    outer_copy(0, targets[0]).start()
-    outer_copy(1, targets[1]).start()
-    spread_copy(1 + c, 0, sibling).start()
+    targets.append(sibling)
+    outer = 3 * (1 - c)
+
+    def spread_copy(half, n):
+        rows = pl.ds(pl.multiple_of(half * NX * HALF, HALF), NX * HALF)
+        block, slot = (1 + c, 2) if n == 2 else (outer, c)
+        return pltpu.make_async_remote_copy(
+            src_ref=window.at[1 + c, rows], dst_ref=window.at[block, rows],
+            send_sem=spread_ssem.at[half, n], recv_sem=spread_rsem.at[half, slot],
+            device_id=targets[n], device_id_type=MESH,
+        )
+
+    for far_half_too in (0, 1):
+        for n, (i, j) in enumerate(moves):
+            if j == far_half_too:
+                from_x, from_zh = wrap(x - i, NX), wrap(zh - j, 2)
+                gather_copy(from_x, from_zh, x, zh, n, from_zh * NX + from_x).wait_recv()
+        for n in range(3):
+            spread_copy(wrap(zh + far_half_too, 2), n).start()
 
     pltpu.make_async_copy(far_half, far_half, acts_sems.at[0]).wait()
     vg_copy.wait_send()
@@ -351,29 +360,47 @@
             for sub in range(2):
                 ring_copy(flow, step, sub).wait_send()
     for i in range(1, RING):
-        zx_copy(wrap(z + i, NZ), z, i).wait_send()
-        yx_copy(wrap(y + i, NY), y, i).wait_send()
+        zx_copy(wrap(z + i, NZ), z).wait_send()
+        yx_copy(wrap(y + i, NY), y).wait_send()
     for i in range(1, NX):
         x_copy(wrap(x + i, NX), x, i).wait_send()
     for n, (i, j) in enumerate(moves):
         gather_copy(x, zh, wrap(x + i, NX), wrap(zh + j, 2), n, zh * NX + x).wait_send()
 
-    pltpu.make_async_copy(window.at[2 - c], window.at[2 - c], spread_rsem.at[0]).wait()
-    pltpu.make_async_copy(window.at[3], window.at[3], spread_rsem.at[1]).wait()
-    pltpu.make_async_copy(window.at[0], window.at[0], spread_rsem.at[2]).wait()
-    first_row = table_ref[0, 0] - (2 * BLOCK * fsdp - BLOCK)
-    columns = jnp.concatenate([window[block] for block in range(4)], axis=1)
-    for start in range(0, slot_ref.shape[0], HALF):
-        row = start + lax.broadcasted_iota(jnp.int32, (HALF, 4 * BLOCK), 0)
-        source = lax.broadcasted_iota(jnp.int32, (HALF, 4 * BLOCK), 1)
-        chosen = (source == row + first_row) & (row < table_ref[0, 1])
-        slot_ref[start : start + HALF, :] = nt_dot(
-            jnp.where(chosen, 1.0, 0.0).astype(BF16), columns
-        ).astype(BF16)
-
-    outer_copy(0, targets[0]).wait_send()
-    outer_copy(1, targets[1]).wait_send()
-    spread_copy(1 + c, 0, sibling).wait_send()
+    def ordered(block):
+        parts = [
+            window[block, (h * NX + g) * HALF : (h * NX + g + 1) * HALF, :]
+            for g in range(NX)
+            for h in range(2)
+        ]
+        return jnp.concatenate(parts, axis=0)
+
+    def picked(start, blocks):
+        columns = jnp.concatenate([ordered(block) for block in blocks], axis=1)
+        part = jnp.concatenate(
+            [chosen_buf[pl.ds(start, HALF), pl.ds(block * BLOCK, BLOCK)] for block in blocks],
+            axis=1,
+        )
+        return nt_dot(part, columns)
+
+    def arrived(block, slot):
+        for half in range(2):
+            part = window.at[block, pl.ds(half * NX * HALF, NX * HALF)]
+            pltpu.make_async_copy(part, part, spread_rsem.at[half, slot]).wait()
+
+    starts = range(0, slot_ref.shape[0], HALF)
+    arrived(2 - c, 2)
+    for start in starts:
+        slot_buf[pl.ds(start, HALF), :] = picked(start, (1, 2))
+    arrived(3, 0)
+    arrived(0, 1)
+    for start in starts:
+        rows = pl.ds(start, HALF)
+        slot_ref[rows, :] = (slot_buf[rows, :] + picked(start, (0, 3))).astype(BF16)
+
+    for half in range(2):
+        for n in range(3):
+            spread_copy(half, n).wait_send()
 
 
 def shards(activations, queries, keys, values, out_grad, positions, shard_table):
@@ -409,9 +436,11 @@
             pltpu.VMEM((NX, HALF, BLOCK), BF16),
             pltpu.VMEM((NX, HALF, BLOCK), BF16),
             pltpu.VMEM((4, width, BLOCK), BF16),
+            pltpu.VMEM((slot_rows, 4 * BLOCK), BF16),
+            pltpu.VMEM((slot_rows, width), F32),
             dma((10,)), dma((1,)), dma((2,)), dma((2,)), dma(ring), dma(ring),
             dma((RING,)), dma((RING,)), dma((RING,)), dma((RING,)), dma((NX,)), dma((NX,)),
-            dma((RING,)), dma((RING,)), dma((3,)), dma((3,)),
+            dma((RING,)), dma((RING,)), dma((2, 3)), dma((2, 3)),
         ],
         compiler_params=pltpu.CompilerParams(
             collective_id=0, has_side_effects=True, vmem_limit_bytes=62 * 1024 * 1024

time: 72.5 us -> 68.8 us (0.949)
  Pallas kernels: 70.4 us -> 66.6 us
    pallas_call x1, Pallas kernels: 70.4 us -> 66.6 us  [shards(): pl.pallas_call(kernel, out_shape=(pltpu.VMEM((tokens, width), BF16), pltp...]
where the time goes in v4:
time: 68.8 us; the launch traced here: 68.6 us
  Pallas kernels  66.6 us (97%)
  local copies, waits for them, and re-layouts  1.38 us (2%)
    pallas_call x1, Pallas kernels, shards(): pl.pallas_call(kernel, out_shape=(pltpu.VMEM((tokens, width), BF16), pltp...  66.6 us
    unnamed x2, local copies, waits for them, and re-layouts  1.38 us

profile of v4, /device:TPU:1, one launch (start us, length us, event | category | flops | bytes accessed | tf_op | source)
XLA Modules:
  0.0 68.6 jit_solution(13198424914347588105)
XLA Ops:
  0.6 66.6 %shard_map.86 = (bf16[128,512]{1,0:T(8,128)(2,1)S(1)}, bf16[320,512]{1,0:T(8,128)(2,1)S(1)}) custom-call(s32[1,2]{1,0:T(1,128)} %bitcast.4, s32[1,128]{1,0:T(1,128)} %bitcast.5, bf16[128,4096]{1,0:T(8,128)(2,1)} %q_hbm.1, bf16[128,512]{1,0:T(8,128)(2,1)} %k_hbm.1, bf16[128,512]{1,0:T(8,128)(2,1)} %v_hbm.1, bf16[128,4096]{1,0:T(8,128)(2,1)} %g_hbm.1, ...), custom_call_target="tpu_custom_call" | custom-call | flops 2000000000 | bytes 6291456 | tf_op jit(solution)/shard_map/pallas_call | solution.py:414
  67.2 0.7 copy.11
  67.9 0.7 %copy.12 = bf16[1,1,320,512]{3,2,1,0:T(8,128)(2,1)} copy(bf16[1,1,320,512]{3,2,1,0:T(8,128)(2,1)S(1)} %bitcast.3) | data formatting | bytes 655360

commit v5 on v4

--- a/solution.py
+++ b/solution.py
@@ -14,6 +14,7 @@
 RING = 8
 BLOCK = 128
 HALF = 64
+PICK = 160
 BF16, F32 = jnp.bfloat16, jnp.float32
 MESH = pl.DeviceIdType.MESH
 AXES = ("y", "y", "z", "z")
@@ -151,10 +152,6 @@
 
     pl.semaphore_wait(barrier, len(partners))
 
-    @pl.loop(0, f_count)
-    def _(f):
-        send_acts(f).start()
-
     vg_copy = pltpu.make_async_remote_copy(
         src_ref=vgt_buf.at[:, pl.ds(0, BLOCK)],
         dst_ref=vgt_buf.at[:, pl.ds(BLOCK, BLOCK)],
@@ -164,6 +161,11 @@
         device_id_type=MESH,
     )
     vg_copy.start()
+
+    @pl.loop(0, f_count)
+    def _(f):
+        send_acts(f).start()
+
     own_half = acts_buf.at[:, pl.ds(0, BLOCK)]
     far_half = acts_buf.at[:, pl.ds(BLOCK, BLOCK)]
     pltpu.make_async_copy(own_half, own_half, local_sem.at[0]).wait()
@@ -288,29 +290,30 @@
             total += jnp.dot(score_grads, stacked(q_ref, first), preferred_element_type=F32)
         key_ref[:, columns] = (total * factor).astype(BF16)
 
+    def x_copy(to, slot):
+        return pltpu.make_async_remote_copy(
+            src_ref=x_send.at[to], dst_ref=x_recv.at[slot],
+            send_sem=x_ssem.at[to], recv_sem=x_rsem.at[slot],
+            device_id=device(to, y, z, c), device_id_type=MESH,
+        )
+
+    def pass_on(total, first):
+        x_send[first : first + 2] = total.astype(BF16)
+        for to in (first, first + 1):
+
+            @pl.when(to != x)
+            def _():
+                x_copy(to, x).start()
+
+    for i in range(1, RING):
+        yx_copy(wrap(y + i, NY), wrap(y - i, NY)).wait_recv()
+    pass_on(sum(yx_recv[i].astype(F32) for i in range(RING)), 2)
     for i in range(1, RING):
         zx_copy(wrap(z + i, NZ), wrap(z - i, NZ)).wait_recv()
-        yx_copy(wrap(y + i, NY), wrap(y - i, NY)).wait_recv()
-    zx_total = zx_recv[0].astype(F32)
-    yx_total = yx_recv[0].astype(F32)
-    for i in range(1, RING):
-        zx_total += zx_recv[i].astype(F32)
-        yx_total += yx_recv[i].astype(F32)
-    x_send[0:2] = zx_total.astype(BF16)
-    x_send[2:4] = yx_total.astype(BF16)
-
-    def x_copy(to, slot, i):
-        return pltpu.make_async_remote_copy(
-            src_ref=x_send.at[to], dst_ref=x_recv.at[slot],
-            send_sem=x_ssem.at[i], recv_sem=x_rsem.at[slot],
-            device_id=device(to, y, z, c), device_id_type=MESH,
-        )
-
-    for i in range(1, NX):
-        x_copy(wrap(x + i, NX), x, i).start()
+    pass_on(sum(zx_recv[i].astype(F32) for i in range(RING)), 0)
     x_recv[x] = x_send[x]
     for i in range(1, NX):
-        x_copy(wrap(x + i, NX), wrap(x - i, NX), i).wait_recv()
+        x_copy(wrap(x + i, NX), wrap(x - i, NX)).wait_recv()
     final = x_recv[0].astype(F32)
     for i in range(1, NX):
         final += x_recv[i].astype(F32)
@@ -326,7 +329,7 @@
 
     own_rows = pl.ds(pl.multiple_of((zh * NX + x) * HALF, HALF), HALF)
     window[1 + c, own_rows] = final.astype(BF16)
-    moves = [(i, j) for j in (1, 0) for i in range(NX) if i or j]
+    moves = [(i, j) for j in (1, 0) for i in (2, 1, 3, 0) if i or j]
     for n, (i, j) in enumerate(moves):
         to_x, to_zh = wrap(x + i, NX), wrap(zh + j, 2)
         gather_copy(x, zh, to_x, to_zh, n, zh * NX + x).start()
@@ -363,7 +366,7 @@
         zx_copy(wrap(z + i, NZ), z).wait_send()
         yx_copy(wrap(y + i, NY), y).wait_send()
     for i in range(1, NX):
-        x_copy(wrap(x + i, NX), x, i).wait_send()
+        x_copy(wrap(x + i, NX), x).wait_send()
     for n, (i, j) in enumerate(moves):
         gather_copy(x, zh, wrap(x + i, NX), wrap(zh + j, 2), n, zh * NX + x).wait_send()
 
@@ -378,7 +381,7 @@
     def picked(start, blocks):
         columns = jnp.concatenate([ordered(block) for block in blocks], axis=1)
         part = jnp.concatenate(
-            [chosen_buf[pl.ds(start, HALF), pl.ds(block * BLOCK, BLOCK)] for block in blocks],
+            [chosen_buf[pl.ds(start, PICK), pl.ds(block * BLOCK, BLOCK)] for block in blocks],
             axis=1,
         )
         return nt_dot(part, columns)
@@ -388,14 +391,14 @@
             part = window.at[block, pl.ds(half * NX * HALF, NX * HALF)]
             pltpu.make_async_copy(part, part, spread_rsem.at[half, slot]).wait()
 
-    starts = range(0, slot_ref.shape[0], HALF)
+    starts = range(0, slot_ref.shape[0], PICK)
     arrived(2 - c, 2)
     for start in starts:
-        slot_buf[pl.ds(start, HALF), :] = picked(start, (1, 2))
+        slot_buf[pl.ds(start, PICK), :] = picked(start, (1, 2))
     arrived(3, 0)
     arrived(0, 1)
     for start in starts:
-        rows = pl.ds(start, HALF)
+        rows = pl.ds(start, PICK)
         slot_ref[rows, :] = (slot_buf[rows, :] + picked(start, (0, 3))).astype(BF16)
 
     for half in range(2):

time: 68.8 us -> 68.2 us (level)
  no operation moved by 1% of the time
where the time goes in v5:
time: 68.2 us; the launch traced here: 68 us
  Pallas kernels  66 us (97%)
  local copies, waits for them, and re-layouts  1.38 us (2%)
    pallas_call x1, Pallas kernels, shards(): pl.pallas_call(kernel, out_shape=(pltpu.VMEM((tokens, width), BF16), pltp...  66 us
    unnamed x2, local copies, waits for them, and re-layouts  1.38 us

profile of v5, /device:TPU:1, one launch (start us, length us, event | category | flops | bytes accessed | tf_op | source)
XLA Modules:
  0.0 68.0 jit_solution(5139495096031897361)
XLA Ops:
  0.6 66.0 %shard_map.86 = (bf16[128,512]{1,0:T(8,128)(2,1)S(1)}, bf16[320,512]{1,0:T(8,128)(2,1)S(1)}) custom-call(s32[1,2]{1,0:T(1,128)} %bitcast.4, s32[1,128]{1,0:T(1,128)} %bitcast.5, bf16[128,4096]{1,0:T(8,128)(2,1)} %q_hbm.1, bf16[128,512]{1,0:T(8,128)(2,1)} %k_hbm.1, bf16[128,512]{1,0:T(8,128)(2,1)} %v_hbm.1, bf16[128,4096]{1,0:T(8,128)(2,1)} %g_hbm.1, ...), custom_call_target="tpu_custom_call" | custom-call | flops 2000000000 | bytes 6291456 | tf_op jit(solution)/shard_map/pallas_call | solution.py:417
  66.6 0.7 copy.11
  67.3 0.7 %copy.12 = bf16[1,1,320,512]{3,2,1,0:T(8,128)(2,1)} copy(bf16[1,1,320,512]{3,2,1,0:T(8,128)(2,1)S(1)} %bitcast.3) | data formatting | bytes 655360

commit v6 on v5

--- a/solution.py
+++ b/solution.py
@@ -142,6 +142,12 @@
     def _(g):
         values_of(g)
 
+    pl.semaphore_wait(barrier, len(partners))
+
+    @pl.loop(0, f_count)
+    def _(f):
+        send_acts(f).start()
+
     for g in range(2, KV_HEADS):
         load_queries[g].wait()
         load_grads[g].wait()
@@ -150,7 +156,6 @@
     def _(g):
         values_of(g)
 
-    pl.semaphore_wait(barrier, len(partners))
 
     vg_copy = pltpu.make_async_remote_copy(
         src_ref=vgt_buf.at[:, pl.ds(0, BLOCK)],
@@ -161,10 +166,6 @@
         device_id_type=MESH,
     )
     vg_copy.start()
-
-    @pl.loop(0, f_count)
-    def _(f):
-        send_acts(f).start()
 
     own_half = acts_buf.at[:, pl.ds(0, BLOCK)]
     far_half = acts_buf.at[:, pl.ds(BLOCK, BLOCK)]

time: 68.2 us -> 66.9 us (0.981)
  Pallas kernels: 66 us -> 64.7 us
    pallas_call x1, Pallas kernels: 66 us -> 64.7 us  [shards(): pl.pallas_call(kernel, out_shape=(pltpu.VMEM((tokens, width), BF16), pltp...]
where the time goes in v6:
time: 66.9 us; the launch traced here: 66.7 us
  Pallas kernels  64.7 us (97%)
  local copies, waits for them, and re-layouts  1.38 us (2%)
    pallas_call x1, Pallas kernels, shards(): pl.pallas_call(kernel, out_shape=(pltpu.VMEM((tokens, width), BF16), pltp...  64.7 us
    unnamed x2, local copies, waits for them, and re-layouts  1.38 us

profile of v6, /device:TPU:1, one launch (start us, length us, event | category | flops | bytes accessed | tf_op | source)
XLA Modules:
  0.0 66.7 jit_solution(2834670059052943387)
XLA Ops:
  0.6 64.7 %shard_map.86 = (bf16[128,512]{1,0:T(8,128)(2,1)S(1)}, bf16[320,512]{1,0:T(8,128)(2,1)S(1)}) custom-call(s32[1,2]{1,0:T(1,128)} %bitcast.4, s32[1,128]{1,0:T(1,128)} %bitcast.5, bf16[128,4096]{1,0:T(8,128)(2,1)} %q_hbm.1, bf16[128,512]{1,0:T(8,128)(2,1)} %k_hbm.1, bf16[128,512]{1,0:T(8,128)(2,1)} %v_hbm.1, bf16[128,4096]{1,0:T(8,128)(2,1)} %g_hbm.1, ...), custom_call_target="tpu_custom_call" | custom-call | flops 2000000000 | bytes 6291456 | tf_op jit(solution)/shard_map/pallas_call | solution.py:418
  65.3 0.7 copy.11
  66.0 0.7 %copy.12 = bf16[1,1,320,512]{3,2,1,0:T(8,128)(2,1)} copy(bf16[1,1,320,512]{3,2,1,0:T(8,128)(2,1)S(1)} %bitcast.3) | data formatting | bytes 655360
